TPU v7x, 512 devices: a whole 4x8x8 slice. The times are simulated.
512 devices in a mesh: ctx: 32 (over x_hi, z, core), tp: 16 (over y, x_lo).
Axes of the slice: x: 4 (x_hi: 2, x_lo: 2; x = x_hi * 2 + x_lo), y: 8, z: 8, core: 2. Of those that a mesh axis runs over, the one named last changes fastest.
Arguments:
- hidden: bfloat16 [12288, 8192], P('ctx', 'tp'), may hold values from -18 to 18
- counts: int32 [32], P('ctx'), may hold values from 1 to 384, 4096 in all
- positions: int32 [12288], P('ctx'), may hold values from 0 to 61439, as said below
- w_query: bfloat16 [8192, 4096], P('ctx', 'tp'), may hold values from -0.0625 to 0.0625
- key_value_weight: bfloat16 [8192, 1024], P('tp'), may hold values from -0.0625 to 0.0625
Outputs:
- attended: bfloat16 [4096, 4096], P('ctx', 'tp')
Inputs may be any that keep to these rules, and one draw needn't show every extreme that they name: The counts sum to 4096; the largest is exactly 384. `positions`: strictly increasing along the array, consecutive entries 1 to 9 apart, the first 0.
All inputs are finite; a program needn't handle non-finite values. No bound on the sum of `counts` on one device may be relied on, other than what follows from the above.
Results may differ from a plain program's by a relative error of at most 0.035.
Values may be sent and summed in bfloat16 or wider, within the bound.
A program may use at most 64 MiB of HBM per device.

v0:
```python
import math

import jax
import jax.numpy as jnp
from jax import lax
from jax.sharding import PartitionSpec as P

HEAD_SIZE = 128
QUERY_HEADS = 32
KEY_VALUE_HEADS = 4
ROWS_DEV = 128


rope_base = 500000.0
masked_score = -1e30
query_block = 512


def rope_angles(position_list, head_dim):
    half_dim = head_dim // 2
    exponent = jnp.arange(half_dim, dtype=jnp.float32) * (2.0 / head_dim)
    inverse = jnp.power(jnp.float32(rope_base), -exponent)
    return position_list.astype(jnp.float32)[:, None] * inverse[None, :]


def rotate(values, angles):
    half_dim = values.shape[-1] // 2
    cosine = jnp.cos(angles)
    sine_part = jnp.sin(angles)
    leading = values[..., :half_dim]
    trailing = values[..., half_dim:]
    return jnp.concatenate(
        [leading * cosine - trailing * sine_part, trailing * cosine + leading * sine_part], axis=-1
    )


def sources_of(ranks, offsets):
    return jnp.sum((offsets[None, :] <= ranks[:, None]).astype(jnp.int32), axis=1) - 1


def add_rows(left, weight_piece):
    return jnp.dot(left, weight_piece, preferred_element_type=jnp.float32)


def on_device(hidden, counts, positions, w_query, key_value_weight):
    ctx_count = lax.axis_size("ctx")
    tensor_count = lax.axis_size("tp")
    capacity = hidden.shape[0]
    local_width = hidden.shape[1]
    slot_rows = capacity // ctx_count
    kept_total = ROWS_DEV * ctx_count
    all_counts = lax.all_gather(counts, "ctx", axis=0, tiled=True)
    offsets = jnp.cumsum(all_counts) - all_counts
    my_index = lax.axis_index("ctx")
    own_offset = offsets[my_index]
    block_index = jnp.arange(slot_rows, dtype=jnp.int32)[:, None]
    target_index = jnp.arange(ctx_count, dtype=jnp.int32)[None, :]
    send_slots = (block_index * ctx_count + (target_index - own_offset) % ctx_count).reshape(-1)
    outgoing = hidden[send_slots].reshape(slot_rows, ctx_count, local_width)
    outgoing_positions = positions[send_slots].reshape(slot_rows, ctx_count)
    incoming, incoming_positions = (
        lax.all_to_all(outgoing, "ctx", split_axis=1, concat_axis=1, tiled=True),
        lax.all_to_all(outgoing_positions, "ctx", split_axis=1, concat_axis=1, tiled=True),
    )
    my_ranks = my_index + ctx_count * jnp.arange(ROWS_DEV, dtype=jnp.int32)
    my_source = sources_of(my_ranks, offsets)
    within = my_ranks - offsets[my_source]
    pick = within // ctx_count * ctx_count + my_source
    local_rows = incoming.reshape(slot_rows * ctx_count, local_width)[pick]
    my_positions = incoming_positions.reshape(slot_rows * ctx_count)[pick]
    key_order = jnp.arange(kept_total, dtype=jnp.int32)
    key_ranks = key_order % ROWS_DEV * ctx_count + key_order // ROWS_DEV
    full_rows = lax.all_gather(local_rows, "tp", axis=1, tiled=True)
    query_head_rows = w_query.shape[1] // HEAD_SIZE
    group_width = QUERY_HEADS // KEY_VALUE_HEADS
    queries = add_rows(full_rows, lax.all_gather(w_query, "ctx", axis=0, tiled=True))
    weight_rows = key_value_weight.shape[0]
    per_head = key_value_weight.reshape(weight_rows, KEY_VALUE_HEADS, 2 * HEAD_SIZE)
    peer_groups = jnp.arange(tensor_count, dtype=jnp.int32) * query_head_rows // group_width
    outgoing_columns = jnp.take(per_head, peer_groups, axis=1)
    arrived = lax.all_to_all(outgoing_columns, "tp", split_axis=1, concat_axis=1, tiled=True)
    feature_blocks = full_rows.reshape(ROWS_DEV, tensor_count, weight_rows)
    key_value_rows = jnp.einsum(
        "isr,rsc->ic", feature_blocks, arrived, preferred_element_type=jnp.float32
    )
    angles = rope_angles(my_positions, HEAD_SIZE)
    queries = rotate(
        queries.reshape(ROWS_DEV, query_head_rows, HEAD_SIZE), angles[:, None, :]
    ).astype(jnp.bfloat16)
    own_keys = rotate(key_value_rows[:, :HEAD_SIZE], angles).astype(jnp.bfloat16)
    own_values = key_value_rows[:, HEAD_SIZE:].astype(jnp.bfloat16)
    query_matrix = queries.transpose(1, 0, 2).reshape(query_head_rows * ROWS_DEV, HEAD_SIZE)
    query_ranks = jnp.tile(my_ranks, query_head_rows)
    score_scale = 1.0 / math.sqrt(HEAD_SIZE)
    stacked_rows = query_head_rows * ROWS_DEV
    block_rows = min(query_block, stacked_rows)
    block_count = stacked_rows // block_rows
    query_blocks = query_matrix.reshape(block_count, block_rows, HEAD_SIZE)
    rank_blocks = query_ranks.reshape(block_count, block_rows)
    all_keys, all_values = (
        lax.all_gather(own_keys, "ctx", axis=0, tiled=True),
        lax.all_gather(own_values, "ctx", axis=0, tiled=True),
    )

    def one_block(pair):
        query_part, rank_part = pair
        causal = key_ranks[None, :] <= rank_part[:, None]
        scores = (
            lax.dot_general(
                query_part, all_keys, (((1,), (1,)), ((), ())), preferred_element_type=jnp.float32
            )
            * score_scale
        )
        scores = jnp.where(causal, scores, masked_score)
        largest = jnp.max(scores, axis=1, keepdims=True)
        weights = jnp.where(causal, jnp.exp(scores - largest), 0.0)
        totals = jnp.sum(weights, axis=1, keepdims=True)
        return (
            jnp.dot(weights.astype(jnp.bfloat16), all_values, preferred_element_type=jnp.float32)
            / totals
        )

    mixed = lax.map(one_block, (query_blocks, rank_blocks)).reshape(stacked_rows, HEAD_SIZE)
    mixed = mixed.astype(jnp.bfloat16)
    return (
        mixed.reshape(query_head_rows, ROWS_DEV, HEAD_SIZE)
        .transpose(1, 0, 2)
        .reshape(ROWS_DEV, query_head_rows * HEAD_SIZE)
    )


def solution(mesh):
    return jax.shard_map(
        on_device,
        mesh=mesh,
        in_specs=(P("ctx", "tp"), P("ctx"), P("ctx"), P("ctx", "tp"), P("tp", None)),
        out_specs=P("ctx", "tp"),
        check_vma=False,
    )
```

profile of v0, /device:TPU:1, one launch (start us, length us, event | category | flops | bytes accessed | tf_op | source)
XLA Modules:
  0.0 482.6 jit_solution(8725383413231738377)
XLA Ops:
  6.5 0.0 copy-start
  7.2 1.3 dynamic-slice
  8.5 0.8 dynamic-update-slice
  9.3 21.7 %all-reduce = s32[32]{0:T(128)S(1)} all-reduce(s32[32]{0:T(128)S(1)} %dynamic-update-slice), channel_id=1, replica_groups=mesh['ctx'=32,'tp'=16] {'ctx'}, use_global_device_ids=true, to_apply=%add | all-reduce | flops 32 | bytes 256
  30.9 0.1 copy.34
  31.0 0.1 reduce-window.9
  31.1 0.1 reduce
  31.2 0.6 dynamic_slice.9
  31.8 0.7 and_select_fusion.3
  32.5 0.1 broadcast_add_fusion
  32.5 0.1 add.198
  32.6 0.0 copy-done
  32.7 2.1 gather_fusion
  34.7 0.0 copy-start.4
  34.7 1.0 copy.35
  35.8 7.5 %all-to-all-start = ((bf16[12,32,512]{2,0,1:T(8,128)(2,1)}), bf16[12,32,512]{2,0,1:T(8,128)(2,1)S(1)}, u32[]{:S(2)}, u32[]{:S(2)}) async-start(bf16[12,32,512]{2,0,1:T(8,128)(2,1)} %copy.35), calls=%async_computation | async-start | bytes 1048576 | tf_op jit(solution)/shard_map/all_to_all | solution.py:62
  43.2 0.0 all-gather.12.cloned.1.call-start
  43.3 0.1 convert_reduce_fusion
  43.4 0.4 copy-done.6
  43.8 1.2 gather_fusion.1
  45.1 16.4 %all-to-all-done = bf16[12,32,512]{2,0,1:T(8,128)(2,1)S(1)} async-done(((bf16[12,32,512]{2,0,1:T(8,128)(2,1)}), bf16[12,32,512]{2,0,1:T(8,128)(2,1)S(1)}, u32[]{:S(2)}, u32[]{:S(2)}) %all-to-all-start) | async-done | bytes 393248 | tf_op jit(solution)/shard_map/all_to_all | solution.py:62
  61.5 0.2 copy.36
  61.7 1.5 gather_fusion.2
  63.2 0.0 all-gather.12.cloned.1.call-update
  63.2 2.8 gather_fusion.3
  66.0 0.1 all_to_all.13
  66.1 0.7 copy.38
  66.8 5.6 %all-to-all-start.1 = ((s32[12,32,1]{0,2,1:T(1,128)}), s32[12,32,1]{0,2,1:T(1,128)S(1)}, u32[]{:S(2)}, u32[]{:S(2)}) async-start(s32[12,32,1]{0,2,1:T(1,128)} %copy.38), calls=%async_computation.1 | async-start | bytes 32768 | tf_op jit(solution)/shard_map/all_to_all | solution.py:63
  72.4 0.0 copy-done.4
  72.4 0.5 copy.42
  72.9 0.0 copy-done.5
  72.9 0.5 copy.43
  73.5 2.8 gather_fusion.5
  76.3 4.6 select_bitcast_fusion
  80.9 0.8 all-to-all-done.1
  81.7 7.0 %all-to-all-start.2 = ((bf16[512,16,256]{2,0,1:T(8,128)(2,1)}), bf16[512,16,256]{2,0,1:T(8,128)(2,1)}, u32[]{:S(2)}, u32[]{:S(2)}) async-start(bf16[512,16,256]{2,0,1:T(8,128)(2,1)} %select_bitcast_fusion), calls=%async_computation.2 | async-start | bytes 8388608 | tf_op jit(solution)/shard_map/all_to_all | solution.py:81
  88.8 0.0 all-gather.6.cloned.1.call-start
  88.8 0.7 all-gather.6.cloned.1.call-update
  89.5 0.0 all-gather.8.cloned.1.call-start
  89.6 0.1 copy.39
  89.7 0.1 reshape.380
  89.7 1.4 gather_fusion.4
  91.1 102.9 %all-gather.12.cloned.1.call-done = bf16[128,8192]{1,0:T(8,128)(2,1)} async-done(((bf16[128,512]{1,0:T(8,128)(2,1)}), bf16[128,8192]{1,0:T(8,128)(2,1)}) %all-gather.12.cloned.1.call-update) | async-done | bytes 2097168 | tf_op jit(solution)/shard_map/all_gather | solution.py:73
  194.1 4.1 copy.41
  198.2 0.0 all-to-all-done.2
  198.2 3.8 convolution_bitcast_fusion
  202.0 0.3 subtract_convert_fusion.1
  202.3 0.7 pad_maximum_fusion.1
  203.0 0.0 all-gather.8.cloned.1.call-update
  203.0 0.0 all-gather.10.cloned.1.call-start
  203.1 0.6 slice.46
  203.7 0.0 all-gather.10.cloned.1.call-update
  203.8 101.6 %all-gather.6.cloned.1.call-done = bf16[8192,256]{1,0:T(8,128)(2,1)} async-done(((bf16[256,256]{1,0:T(8,128)(2,1)}), bf16[8192,256]{1,0:T(8,128)(2,1)}) %all-gather.6.cloned.1.call-update) | async-done | bytes 4194320 | tf_op jit(solution)/shard_map/all_gather | solution.py:76
  305.4 2.9 fusion.28
  308.3 0.1 reshape.379
  308.4 0.2 fusion.26
  308.6 0.1 pad_maximum_fusion
  308.7 79.9 %all-gather.8.cloned.1.call-done = bf16[4096,128]{1,0:T(8,128)(2,1)} async-done(((bf16[128,128]{1,0:T(8,128)(2,1)}), bf16[4096,128]{1,0:T(8,128)(2,1)}) %all-gather.8.cloned.1.call-update) | async-done | bytes 1048592 | tf_op jit(solution)/shard_map/all_gather | solution.py:101
  388.6 2.1 fusion.27
  390.7 1.9 copy-done.3
  392.7 1.0 fusion.1
  393.7 78.3 %all-gather.10.cloned.1.call-done = bf16[4096,128]{1,0:T(8,128)(2,1)} async-done(((bf16[128,128]{1,0:T(8,128)(2,1)}), bf16[4096,128]{1,0:T(8,128)(2,1)}) %all-gather.10.cloned.1.call-update) | async-done | bytes 1048592 | tf_op jit(solution)/shard_map/all_gather | solution.py:102
  472.0 3.4 fusion.8
  475.4 0.6 copy.55
  (27 shorter events, 0.2 us)
Async XLA Ops:
  6.5 26.1 %copy-start = (bf16[384,512]{1,0:T(8,128)(2,1)S(1)}, bf16[384,512]{1,0:T(8,128)(2,1)}, u32[]{:S(2)}) copy-start(bf16[384,512]{1,0:T(8,128)(2,1)} %param.5) | copy-start | bytes 1179652
  30.9 32.3 %copy-start.1 = (s32[384]{0:T(512)S(1)}, s32[384]{0:T(512)}, u32[]{:S(2)}) copy-start(s32[384]{0:T(512)} %param.7) | copy-start | bytes 4612
  34.7 37.6 %copy-start.4 = (bf16[512,1024]{1,0:T(8,128)(2,1)S(1)}, bf16[512,1024]{1,0:T(8,128)(2,1)}, u32[]{:S(2)}) copy-start(bf16[512,1024]{1,0:T(8,128)(2,1)} %param.9) | copy-start | bytes 3145732
  35.8 25.7 %all-to-all-start = ((bf16[12,32,512]{2,0,1:T(8,128)(2,1)}), bf16[12,32,512]{2,0,1:T(8,128)(2,1)S(1)}, u32[]{:S(2)}, u32[]{:S(2)}) async-start(bf16[12,32,512]{2,0,1:T(8,128)(2,1)} %copy.35), calls=%async_computation | async-start | bytes 1048576 | tf_op jit(solution)/shard_map/all_to_all | solution.py:62
  43.2 150.8 %all-gather.12.cloned.1.call-start = ((), (), s32[]{:S(2)}) async-start(), calls=%async_computation.6 | async-start | bytes 2228224 | tf_op jit(solution)/shard_map/all_gather | solution.py:73
  43.3 0.5 copy-start.6
  45.1 27.8 %copy-start.5 = (s32[1024]{0:T(1024)}, s32[1024]{0:T(1024)S(1)}, u32[]{:S(2)}) copy-start(s32[1024]{0:T(1024)S(1)} %pad_clamp_fusion.1) | copy-start | bytes 12292
  66.8 14.9 %all-to-all-start.1 = ((s32[12,32,1]{0,2,1:T(1,128)}), s32[12,32,1]{0,2,1:T(1,128)S(1)}, u32[]{:S(2)}, u32[]{:S(2)}) async-start(s32[12,32,1]{0,2,1:T(1,128)} %copy.38), calls=%async_computation.1 | async-start | bytes 32768 | tf_op jit(solution)/shard_map/all_to_all | solution.py:63
  81.7 116.4 %all-to-all-start.2 = ((bf16[512,16,256]{2,0,1:T(8,128)(2,1)}), bf16[512,16,256]{2,0,1:T(8,128)(2,1)}, u32[]{:S(2)}, u32[]{:S(2)}) async-start(bf16[512,16,256]{2,0,1:T(8,128)(2,1)} %select_bitcast_fusion), calls=%async_computation.2 | async-start | bytes 8388608 | tf_op jit(solution)/shard_map/all_to_all | solution.py:81
  88.8 216.6 %all-gather.6.cloned.1.call-start = ((), (), s32[]{:S(2)}) async-start(), calls=%async_computation.3 | async-start | bytes 4325376 | tf_op jit(solution)/shard_map/all_gather | solution.py:76
  89.5 299.1 %all-gather.8.cloned.1.call-start = ((), (), s32[]{:S(2)}) async-start(), calls=%async_computation.4 | async-start | bytes 1081344 | tf_op jit(solution)/shard_map/all_gather | solution.py:101
  198.2 5.6 %copy-start.7 = (s32[128]{0:T(128)S(1)}, s32[128]{0:T(128)}, u32[]{:S(2)}) copy-start(s32[128]{0:T(128)} %copy-done.6) | copy-start | bytes 1540
  198.2 107.2 %copy-start.2 = (bf16[128,8192]{1,0:T(8,128)(2,1)S(1)}, bf16[128,8192]{1,0:T(8,128)(2,1)}, u32[]{:S(2)}) copy-start(bf16[128,8192]{1,0:T(8,128)(2,1)} %all-gather.12.cloned.1.call-done) | copy-start | bytes 6291460
  203.0 269.0 %all-gather.10.cloned.1.call-start = ((), (), s32[]{:S(2)}) async-start(), calls=%async_computation.5 | async-start | bytes 1081344 | tf_op jit(solution)/shard_map/all_gather | solution.py:102
  390.7 2.0 copy-start.3
Sparse Core Ops, SparseCore 0:
  63.3 130.6 all-gather.11
  197.4 107.9 all-gather.5
  308.8 79.7 all-gather.7
  391.8 80.1 all-gather.9
where the time goes:
time: 483 us
  waiting for transfers between devices  381 us (79%)
  local copies, waits for them, and re-layouts  25.8 us (5%)
  blocking collectives  21.7 us (4%)
  starting transfers between devices  20.2 us (4%)
  between operations  14.1 us (3%)
  matrix products  12.2 us (3%)
  other arithmetic  7.89 us (2%)
    all_gather x1, waiting for transfers between devices, on_device(): full_rows = lax.all_gather(local_rows, 'tp', axis=1, tiled=True)  103 us
    all_gather x1, waiting for transfers between devices, on_device(): lax.all_gather(w_query, 'ctx', axis=0, tiled=True)  102 us
    all_gather x1, waiting for transfers between devices, on_device(): lax.all_gather(own_keys, 'ctx', axis=0, tiled=True)  79.9 us
    all_gather x1, waiting for transfers between devices, on_device(): lax.all_gather(own_values, 'ctx', axis=0, tiled=True)  78.3 us
    unnamed x1, blocking collectives  21.7 us
    all_to_all x1, waiting for transfers between devices, on_device(): lax.all_to_all(outgoing, 'ctx', split_axis=1, concat_axis=1, tiled=True)  16.4 us
  transfers between devices with their start and end apart: 7, of which 6 were waited for; matrix products, arithmetic and copies ran while one was open for 6% of the time, Pallas kernels for 0%

commit v1 on v0

v1 whole, which is shorter than its diff:
```python
import math

import jax
import jax.numpy as jnp
from jax import lax
from jax.experimental import pallas as pl
from jax.experimental.pallas import tpu as pltpu
from jax.sharding import PartitionSpec as P

HEAD_SIZE = 128
QUERY_HEADS = 32
KEY_VALUE_HEADS = 4
ROWS_DEV = 128
CAP = 384
N_CTX = 32
N_TP = 16
MESH = pl.DeviceIdType.MESH
rope_base = 500000.0
masked_score = -1e30
BF16 = jnp.bfloat16
F32 = jnp.float32


def iota(shape, dim):
    return lax.broadcasted_iota(jnp.int32, shape, dim)


def kernel(info_ref, inv_ref, hidden_hbm, wq_hbm, kvw_hbm, out_ref,
           info_all, hidden, kvw, outb, inb, xall, wall, kvpart, kvin, kvall, trig, qbuf,
           load_sem, send_sem, info_sem, a2a_sem, w_sem, w_sib, x_sem, rs_sem, kv_sem):
    c = lax.axis_index("ctx")
    t = lax.axis_index("tp")
    xh, z, co = c // 16, lax.rem(c // 2, 8), lax.rem(c, 2)
    y, xl = t // 2, lax.rem(t, 2)
    idx = c // 2
    m = lax.rem(t, 4)

    def ctx_of(h, zz, cc):
        return {"ctx": (h * 8 + zz) * 2 + cc}

    z_right, z_left = ctx_of(xh, lax.rem(z + 1, 8), co), ctx_of(xh, lax.rem(z + 7, 8), co)
    sibling, far_x = ctx_of(xh, z, 1 - co), ctx_of(1 - xh, z, co)
    y_right, y_left = {"tp": lax.rem(y + 1, 8) * 2 + xl}, {"tp": lax.rem(y + 7, 8) * 2 + xl}
    near_x = {"tp": y * 2 + 1 - xl}
    y_pair = {"tp": (y + 1 - 2 * lax.rem(y, 2)) * 2 + xl}

    def send(src, dst, ss, rs, device):
        pltpu.make_async_remote_copy(
            src_ref=src, dst_ref=dst, send_sem=ss, recv_sem=rs, device_id=device, device_id_type=MESH
        ).start()

    def wait(ref, sem):
        pltpu.make_async_copy(ref, ref, sem).wait()

    barrier = pltpu.get_barrier_semaphore()

    @pl.loop(1, N_CTX)
    def _(d):
        pl.semaphore_signal(barrier, inc=1, device_id={"ctx": lax.rem(c + d, N_CTX)}, device_id_type=MESH)

    @pl.loop(1, N_TP)
    def _(d):
        pl.semaphore_signal(barrier, inc=1, device_id={"tp": lax.rem(t + d, N_TP)}, device_id_type=MESH)

    loads = [
        pltpu.make_async_copy(wq_hbm, wall.at[c], load_sem.at[0]),
        pltpu.make_async_copy(hidden_hbm, hidden, load_sem.at[1]),
        pltpu.make_async_copy(kvw_hbm, kvw, load_sem.at[2]),
    ]
    for load in loads:
        load.start()
    info_all[c] = info_ref[...]
    loads[0].wait()
    pl.semaphore_wait(barrier, N_CTX + N_TP - 2)

    @pl.loop(1, N_CTX)
    def _(d):
        send(info_ref, info_all.at[c], send_sem.at[0], info_sem.at[0], {"ctx": lax.rem(c + d, N_CTX)})

    halves = (xh, 1 - xh)

    def w_block(r, zz, cc):
        return wall.at[(halves[r] * 8 + zz) * 2 + cc]

    def w_send(r, zz, device, sem):
        block = w_block(r, zz, co)
        send(block, block, send_sem.at[1], sem, device)

    w_right = (4, 3)

    def w_start(r):
        w_send(r, z, z_right, w_sem.at[r * 8])
        w_send(r, z, z_left, w_sem.at[r * 8 + 4])
        w_send(r, z, sibling, w_sib.at[0])

    def w_step(s):
        for r in range(2):
            if s < w_right[r]:
                zz = lax.rem(z + 7 - s, 8)
                wait(w_block(r, zz, co), w_sem.at[r * 8 + s])
                if s + 1 < w_right[r]:
                    w_send(r, zz, z_right, w_sem.at[r * 8 + s + 1])
                w_send(r, zz, sibling, w_sib.at[0])
            if s < 7 - w_right[r]:
                zz = lax.rem(z + 1 + s, 8)
                wait(w_block(r, zz, co), w_sem.at[r * 8 + 4 + s])
                if s + 1 < 7 - w_right[r]:
                    w_send(r, zz, z_left, w_sem.at[r * 8 + 4 + s + 1])
                w_send(r, zz, sibling, w_sib.at[0])

    w_send(0, z, far_x, w_sem.at[16])
    w_start(0)

    wait(info_all.at[pl.ds(0, N_CTX - 1)], info_sem.at[0])
    counts = info_all[:, 3, :]
    shard = iota((N_CTX, 128), 0)
    own_offset = jnp.sum(jnp.where(shard < c, counts, 0), axis=0, keepdims=True)
    counts_wide = jnp.concatenate([counts] * 4, axis=1)
    shard_wide, column = iota((N_CTX, 512), 0), iota((N_CTX, 512), 1)
    first = jnp.sum(jnp.where(shard_wide < column // 16, counts_wide, 0), axis=0, keepdims=True)
    number = jnp.sum(jnp.where(shard_wide == column // 16, counts_wide, 0), axis=0, keepdims=True)
    lane = iota((N_CTX, 128), 1)
    first_of = jnp.sum(jnp.where(shard < lane, counts, 0), axis=0, keepdims=True)
    number_of = jnp.sum(jnp.where(shard == lane, counts, 0), axis=0, keepdims=True)

    slot = iota((1, CAP), 1)
    place = ((slot + jnp.concatenate([own_offset] * 3, axis=1)) % 32) * 16 + slot // 32
    loads[1].wait()
    for part in range(4):
        chosen = (iota((128, CAP), 0) + 128 * part == place).astype(F32).astype(BF16)
        outb[pl.ds(part * 128, 128)] = jnp.dot(chosen, hidden[...], preferred_element_type=F32).astype(BF16)
    mine = pl.ds(pl.multiple_of(c * 16, 16), 16)
    inb[mine] = outb[mine]

    @pl.loop(1, N_CTX)
    def _(d):
        peer = lax.rem(c + d, N_CTX)
        send(outb.at[pl.ds(pl.multiple_of(peer * 16, 16), 16)], inb.at[mine], send_sem.at[2], a2a_sem.at[0], {"ctx": peer})

    rank = iota((ROWS_DEV, 128), 0) * N_CTX + c
    from_shard = (rank >= first_of) & (rank < first_of + number_of)
    within = jnp.sum(jnp.where(from_shard, rank - first_of, 0).astype(F32), axis=1, keepdims=True)
    source = from_shard.astype(F32).astype(BF16)[:, :N_CTX]
    picked = jnp.zeros((ROWS_DEV, 128), F32)
    for part in range(3):
        place_of = info_all[:, part, :]
        high = jnp.dot(source, (place_of // 256).astype(F32).astype(BF16), preferred_element_type=F32)
        low = jnp.dot(source, (place_of % 256).astype(F32).astype(BF16), preferred_element_type=F32)
        here = iota((ROWS_DEV, 128), 1).astype(F32) + 128.0 * part == within
        picked += jnp.where(here, high * 256.0 + low, 0.0)
    angles = jnp.sum(picked, axis=1, keepdims=True) * inv_ref[0:1, :]
    trig[0] = jnp.cos(angles)
    trig[1] = jnp.where(iota((ROWS_DEV, 128), 1) < HEAD_SIZE // 2, -1.0, 1.0) * jnp.sin(angles)

    def rotate(u, cosine, sine):
        return u * cosine + pltpu.roll(u, HEAD_SIZE // 2, 1) * sine

    pick_rank = iota((ROWS_DEV, 512), 0) * N_CTX + c
    low_rank = first + 32 * (iota((1, 512), 1) % 16)
    high_rank = jnp.minimum(low_rank + 32, first + number)
    pick = ((pick_rank >= low_rank) & (pick_rank < high_rank)).astype(F32).astype(BF16)
    wait(inb.at[pl.ds(0, 16 * (N_CTX - 1))], a2a_sem.at[0])
    rows = jnp.dot(pick, inb[...], preferred_element_type=F32).astype(BF16)
    xall[t] = rows

    sides = (xl, 1 - xl)
    x_right = (4, 3)

    def x_block(r, yy):
        return xall.at[yy * 2 + sides[r]]

    def x_send(r, yy, device, sem):
        block = x_block(r, yy)
        send(block, block, send_sem.at[3], sem, device)

    def x_start(r):
        x_send(r, y, y_right, x_sem.at[r * 8])
        x_send(r, y, y_left, x_sem.at[r * 8 + 4])

    def x_step(s):
        for r in range(2):
            if s < x_right[r]:
                yy = lax.rem(y + 7 - s, 8)
                wait(x_block(r, yy), x_sem.at[r * 8 + s])
                if s + 1 < x_right[r]:
                    x_send(r, yy, y_right, x_sem.at[r * 8 + s + 1])
            if s < 7 - x_right[r]:
                yy = lax.rem(y + 1 + s, 8)
                wait(x_block(r, yy), x_sem.at[r * 8 + 4 + s])
                if s + 1 < 7 - x_right[r]:
                    x_send(r, yy, y_left, x_sem.at[r * 8 + 4 + s + 1])

    x_send(0, y, near_x, x_sem.at[16])
    x_start(0)

    loads[2].wait()
    for g in range(KEY_VALUE_HEADS):
        kvpart[g] = jnp.dot(rows, kvw[:, g * 256:(g + 1) * 256], preferred_element_type=F32).astype(BF16)

    @pl.loop(1, N_TP)
    def _(d):
        peer = lax.rem(t + d, N_TP)
        send(kvpart.at[peer // 4, pl.ds(pl.multiple_of(lax.rem(peer, 4) * 32, 32), 32)], kvin.at[t],
             send_sem.at[4], rs_sem.at[0], {"tp": peer})

    mine_kv = pl.ds(pl.multiple_of(m * 32, 32), 32)
    kvin[t] = kvpart[t // 4, mine_kv]
    wait(x_block(1, y), x_sem.at[16])
    x_start(1)
    wait(w_block(1, z, co), w_sem.at[16])
    w_start(1)
    w_step(0)
    x_step(0)
    w_step(1)

    wait(kvin.at[pl.ds(0, N_TP - 1)], rs_sem.at[0])
    total = jnp.zeros((32, 256), F32)
    for s in range(N_TP):
        total += kvin[s].astype(F32)
    kvall[m, co, idx, :, :HEAD_SIZE] = rotate(total[:, :HEAD_SIZE], trig[0, mine_kv], trig[1, mine_kv]).astype(BF16)
    kvall[m, co, idx, :, HEAD_SIZE:] = total[:, HEAD_SIZE:].astype(BF16)

    @pl.loop(1, 16)
    def _(d):
        block = kvall.at[m, co, idx]
        send(block, block, send_sem.at[5], kv_sem.at[0], {"ctx": lax.rem(idx + d, 16) * 2 + co})

    x_step(1)
    w_step(2)
    x_step(2)
    w_step(3)
    wait(kvall.at[m, co, pl.ds(0, 15)], kv_sem.at[0])

    def kv_send(ref, device, sem):
        send(ref, ref, send_sem.at[6], sem, device)

    mx, my, mxy = m + 1 - 2 * xl, lax.rem(m + 2, 4), 3 - m
    kv_send(kvall.at[m, co], near_x, kv_sem.at[1])
    kv_send(kvall.at[m, co], y_pair, kv_sem.at[2])
    kv_send(kvall.at[m, co], sibling, kv_sem.at[5])
    x_step(3)
    lo_half, hi_half = pl.ds(0, 8), pl.ds(8, 8)
    wait(kvall.at[mx, co], kv_sem.at[1])
    kv_send(kvall.at[mx, co, lo_half], y_pair, kv_sem.at[3])
    kv_send(kvall.at[mx, co], sibling, kv_sem.at[6])
    wait(kvall.at[my, co], kv_sem.at[2])
    kv_send(kvall.at[my, co, hi_half], near_x, kv_sem.at[4])
    kv_send(kvall.at[my, co], sibling, kv_sem.at[7])

    wait(wall.at[pl.ds(0, 16)], w_sib.at[0])

    def add_block(k, acc):
        weight = wall[pl.ds(k * 2, 2)].reshape(512, 256)
        return acc + jnp.dot(xall[k], weight, preferred_element_type=F32)

    q = lax.fori_loop(0, N_TP, add_block, jnp.zeros((ROWS_DEV, 256), F32))
    for head in range(2):
        turned = rotate(q[:, head * 128:(head + 1) * 128], trig[0], trig[1]).astype(BF16)
        for j in range(4):
            qbuf[j, head * 32:(head + 1) * 32, :] = turned[j * 32:(j + 1) * 32]

    wait(kvall.at[mxy, co, lo_half], kv_sem.at[3])
    wait(kvall.at[mxy, co, hi_half], kv_sem.at[4])
    kv_send(kvall.at[mxy, co], sibling, kv_sem.at[8])
    wait(kvall.at[m, 1 - co], kv_sem.at[5])
    wait(kvall.at[mx, 1 - co], kv_sem.at[6])
    wait(kvall.at[my, 1 - co], kv_sem.at[7])
    wait(kvall.at[mxy, 1 - co], kv_sem.at[8])

    scale = 1.0 / math.sqrt(HEAD_SIZE)
    key_index = iota((64, 1024), 1)
    query_row = iota((64, 1024), 0) % 32
    key_row = key_index % 32
    key_ctx = (key_index // 32 % 16) * 2 + key_index // 512
    seen = (key_row < query_row) | ((key_row == query_row) & (key_ctx <= c))
    for j in range(4):
        scores = []
        for b in range(j + 1):
            keys = kvall[b, :, :, :, :HEAD_SIZE].reshape(1024, HEAD_SIZE)
            part = lax.dot_general(qbuf[j], keys, (((1,), (1,)), ((), ())), preferred_element_type=F32) * scale
            scores.append(jnp.where(seen, part, masked_score) if b == j else part)
        largest = jnp.max(scores[0], axis=1, keepdims=True)
        for part in scores[1:]:
            largest = jnp.maximum(largest, jnp.max(part, axis=1, keepdims=True))
        sums = jnp.zeros((64, 1), F32)
        mixed = jnp.zeros((64, HEAD_SIZE), F32)
        for b in range(j + 1):
            weights = jnp.exp(scores[b] - largest)
            if b == j:
                weights = jnp.where(seen, weights, 0.0)
            sums += jnp.sum(weights, axis=1, keepdims=True)
            values = kvall[b, :, :, :, HEAD_SIZE:].reshape(1024, HEAD_SIZE)
            mixed += jnp.dot(weights.astype(BF16), values, preferred_element_type=F32)
        result = (mixed / sums).astype(BF16)
        for head in range(2):
            out_ref[j * 32:(j + 1) * 32, head * 128:(head + 1) * 128] = result[head * 32:(head + 1) * 32]

    wait(info_all.at[pl.ds(0, N_CTX - 1)], send_sem.at[0])
    wait(wall.at[pl.ds(0, 16)], send_sem.at[1])
    wait(wall.at[pl.ds(0, 15)], send_sem.at[1])
    wait(outb.at[pl.ds(0, 16 * (N_CTX - 1))], send_sem.at[2])
    wait(xall.at[pl.ds(0, 15)], send_sem.at[3])
    wait(kvin.at[pl.ds(0, N_TP - 1)], send_sem.at[4])
    wait(kvall.at[m, co, pl.ds(0, 15)], send_sem.at[5])
    wait(kvall.at[pl.ds(0, 3)], send_sem.at[6])
    wait(kvall.at[m, co, pl.ds(0, 8)], send_sem.at[6])
    wait(kvall.at[m, co, pl.ds(0, 8)], send_sem.at[6])


def on_device(hidden, counts, positions, w_query, key_value_weight):
    info = jnp.concatenate(
        [positions.reshape(3, 128), jnp.broadcast_to(counts[:, None], (1, 128)), jnp.zeros((4, 128), jnp.int32)], axis=0
    )
    half = HEAD_SIZE // 2
    exponent = jnp.arange(half, dtype=F32) * (2.0 / HEAD_SIZE)
    inverse = jnp.power(jnp.float32(rope_base), -exponent)
    inverse = jnp.broadcast_to(jnp.concatenate([inverse, inverse])[None, :], (8, 128))
    vmem, anywhere = pl.BlockSpec(memory_space=pltpu.VMEM), pl.BlockSpec(memory_space=pl.ANY)
    dma = pltpu.SemaphoreType.DMA
    return pl.pallas_call(
        kernel,
        out_shape=jax.ShapeDtypeStruct((ROWS_DEV, 256), BF16),
        in_specs=[vmem, vmem, anywhere, anywhere, anywhere],
        out_specs=vmem,
        scratch_shapes=[
            pltpu.VMEM((N_CTX, 8, 128), jnp.int32),
            pltpu.VMEM((CAP, 512), BF16),
            pltpu.VMEM((512, 1024), BF16),
            pltpu.VMEM((512, 512), BF16),
            pltpu.VMEM((512, 512), BF16),
            pltpu.VMEM((N_TP, ROWS_DEV, 512), BF16),
            pltpu.VMEM((N_CTX, 256, 256), BF16),
            pltpu.VMEM((4, ROWS_DEV, 256), BF16),
            pltpu.VMEM((N_TP, 32, 256), BF16),
            pltpu.VMEM((4, 2, 16, 32, 256), BF16),
            pltpu.VMEM((2, ROWS_DEV, 128), F32),
            pltpu.VMEM((4, 64, 128), BF16),
            dma((3,)),
            dma((7,)),
            dma((1,)),
            dma((1,)),
            dma((17,)),
            dma((1,)),
            dma((17,)),
            dma((1,)),
            dma((9,)),
        ],
        compiler_params=pltpu.CompilerParams(
            collective_id=0, has_side_effects=True, vmem_limit_bytes=48 * 1024 * 1024
        ),
        name="gqa",
    )(info, inverse, hidden, w_query, key_value_weight)


def solution(mesh):
    return jax.shard_map(
        on_device,
        mesh=mesh,
        in_specs=(P("ctx", "tp"), P("ctx"), P("ctx"), P("ctx", "tp"), P("tp", None)),
        out_specs=P("ctx", "tp"),
        check_vma=False,
    )
```

time: 483 us -> 89.7 us (0.19)
  waiting for transfers between devices: 381 us -> 0 us
  Pallas kernels: 0 us -> 84.1 us
  blocking collectives: 21.7 us -> 0 us
  local copies, waits for them, and re-layouts: 25.8 us -> 4.5 us
  starting transfers between devices: 20.2 us -> 0 us
  between operations: 14.1 us -> 0.67 us
  matrix products: 12.2 us -> 0 us
  other arithmetic: 7.89 us -> 0.16 us
    all_gather x4 -> x0, waiting for transfers between devices: 363 us -> none  [the longest x1 103 us: on_device(): full_rows = lax.all_gather(local_rows, 'tp', axis=1, tiled=True)]
    pallas_call x0 -> x1, Pallas kernels: none -> 84.1 us  [on_device(): pl.pallas_call(kernel, out_shape=jax.ShapeDtypeStruct((ROWS_DEV, 256), BF...]
    unnamed x1 -> x0, blocking collectives: 21.7 us -> none
    all_to_all x3 -> x0, starting transfers between devices: 20 us -> none  [the longest x1 7.46 us: on_device(): lax.all_to_all(outgoing, 'ctx', split_axis=1, concat_axis=1, tiled=True)]
    all_to_all x3 -> x0, waiting for transfers between devices: 17.2 us -> none  [the longest x1 16.4 us: on_device(): lax.all_to_all(outgoing, 'ctx', split_axis=1, concat_axis=1, tiled=True)]
    dot_general x4 -> x0, matrix products: 12.2 us -> none  [the longest x1 3.81 us: on_device(): jnp.einsum('isr,rsc->ic', feature_blocks, arrived, preferred_element_type...]
    gather x6 -> x0, local copies, waits for them, and re-layouts: 11.8 us -> none  [the longest x1 2.8 us: on_device(): outgoing_positions = positions[send_slots].reshape(slot_rows, ctx_count)]
    select_n x6 -> x0, other arithmetic: 5.33 us -> none  [the longest x2 4.64 us: on_device(): outgoing_columns = jnp.take(per_head, peer_groups, axis=1)]
  transfers between devices with their start and end apart: 7 -> 0, of which waited for: 6 -> 0; matrix products, arithmetic and copies ran while one was open for 6% -> 0% of each run, Pallas kernels for 0% -> 0%
where the time goes in v1:
time: 89.7 us; the launch traced here: 89.4 us
  Pallas kernels  84.1 us (94%)
  local copies, waits for them, and re-layouts  4.5 us (5%)
    pallas_call x1, Pallas kernels, on_device(): pl.pallas_call(kernel, out_shape=jax.ShapeDtypeStruct((ROWS_DEV, 256), BF...  84.1 us
    unnamed x9, local copies, waits for them, and re-layouts  4.35 us

profile of v1, /device:TPU:1, one launch (start us, length us, event | category | flops | bytes accessed | tf_op | source)
XLA Modules:
  0.0 89.4 jit_solution(7642333315288607208)
XLA Ops:
  0.7 0.1 pad.3.clone
  0.7 0.1 pad.4.clone
  0.8 0.0 copy-start.3
  0.8 0.1 pad_maximum_fusion
  0.9 0.6 copy-done.3
  1.5 0.1 add_add_fusion.info_ref
  1.6 0.0 copy-start
  1.6 1.2 %copy-done = bf16[512,1024]{1,0:T(8,128)(2,1)S(1)} copy-done((bf16[512,1024]{1,0:T(8,128)(2,1)S(1)}, bf16[512,1024]{1,0:T(8,128)(2,1)}, u32[]{:S(2)}) %copy-start) | copy-done | bytes 1048600
  2.8 0.0 copy-start.1
  2.8 1.0 %copy-done.1 = bf16[384,512]{1,0:T(8,128)(2,1)S(1)} copy-done((bf16[384,512]{1,0:T(8,128)(2,1)S(1)}, bf16[384,512]{1,0:T(8,128)(2,1)}, u32[]{:S(2)}) %copy-start.1) | copy-done | bytes 393240
  3.8 0.0 copy-start.2
  3.8 0.9 %copy-done.2 = bf16[256,256]{1,0:T(8,128)(2,1)S(1)} copy-done((bf16[256,256]{1,0:T(8,128)(2,1)S(1)}, bf16[256,256]{1,0:T(8,128)(2,1)}, u32[]{:S(2)}) %copy-start.2) | copy-done | bytes 131096
  4.7 84.1 %gqa.1 = bf16[128,256]{1,0:T(8,128)(2,1)S(1)} custom-call(s32[8,128]{1,0:T(8,128)S(1)} %add_add_fusion.info_ref, f32[8,128]{1,0:T(8,128)S(1)} %broadcast_in_dim.20.inv_ref, bf16[384,512]{1,0:T(8,128)(2,1)S(1)} %copy-done.1, bf16[256,256]{1,0:T(8,128)(2,1)S(1)} %copy-done.2, bf16[512,1024]{1,0:T(8,128)(2,1)S(1)} %copy-done), custom_call_target="tpu_custom_call" | custom-call | tf_op jit(solution)/shard_map/gqa/pallas_call | solution.py:320
  88.8 0.6 copy.8
  (3 shorter events, 0.0 us)
Async XLA Ops:
  0.8 0.7 copy-start.3
  1.6 1.2 %copy-start = (bf16[512,1024]{1,0:T(8,128)(2,1)S(1)}, bf16[512,1024]{1,0:T(8,128)(2,1)}, u32[]{:S(2)}) copy-start(bf16[512,1024]{1,0:T(8,128)(2,1)} %kvw_hbm.1) | copy-start | bytes 3145732
  2.8 1.0 %copy-start.1 = (bf16[384,512]{1,0:T(8,128)(2,1)S(1)}, bf16[384,512]{1,0:T(8,128)(2,1)}, u32[]{:S(2)}) copy-start(bf16[384,512]{1,0:T(8,128)(2,1)} %hidden_hbm.1) | copy-start | bytes 1179652
  3.8 0.9 %copy-start.2 = (bf16[256,256]{1,0:T(8,128)(2,1)S(1)}, bf16[256,256]{1,0:T(8,128)(2,1)}, u32[]{:S(2)}) copy-start(bf16[256,256]{1,0:T(8,128)(2,1)} %wq_hbm.1) | copy-start | bytes 393220

commit v2 on v1

v2 whole, which is shorter than its diff:
```python
import math

import jax
import jax.numpy as jnp
import numpy as np
from jax import lax
from jax.experimental import pallas as pl
from jax.experimental.pallas import tpu as pltpu
from jax.sharding import PartitionSpec as P

HEAD_SIZE = 128
QUERY_HEADS = 32
KEY_VALUE_HEADS = 4
ROWS_DEV = 128
CAP = 384
N_CTX = 32
N_TP = 16
MESH = pl.DeviceIdType.MESH
rope_base = 500000.0
masked_score = -1e30
BF16 = jnp.bfloat16
F32 = jnp.float32


def iota(shape, dim):
    return lax.broadcasted_iota(jnp.int32, shape, dim)


def kernel(counts_ref, inv_hbm, pos_hbm, hidden_hbm, wq_hbm, kvw_hbm, out_ref,
           counts_all, pos_all, inv_ref, hidden, kvw, wq, outb, inb, xall, wall, kvfull, kvp, kvx, kvs, kvin, kvall,
           trig, qpart, qin, qbuf,
           load_sem, send_sem, info_sem, pos_sem, a2a_sem, w_sem, w_far, w_sib, x_sem, rs_sem, kv_sem, q_sem):
    c = lax.axis_index("ctx")
    t = lax.axis_index("tp")
    xh, z, co = c // 16, lax.rem(c // 2, 8), lax.rem(c, 2)
    y, xl = t // 2, lax.rem(t, 2)
    idx = c // 2
    m = lax.rem(t, 4)

    def ctx_of(h, zz, cc):
        return {"ctx": (h * 8 + zz) * 2 + cc}

    z_near = (ctx_of(xh, lax.rem(z + 1, 8), co), ctx_of(xh, lax.rem(z + 7, 8), co))
    sibling, far_x = ctx_of(xh, z, 1 - co), ctx_of(1 - xh, z, co)
    y_right, y_left = {"tp": lax.rem(y + 1, 8) * 2 + xl}, {"tp": lax.rem(y + 7, 8) * 2 + xl}
    near_x = {"tp": y * 2 + 1 - xl}
    y_pair = {"tp": (y + 1 - 2 * lax.rem(y, 2)) * 2 + xl}

    def send(src, dst, ss, rs, device):
        pltpu.make_async_remote_copy(
            src_ref=src, dst_ref=dst, send_sem=ss, recv_sem=rs, device_id=device, device_id_type=MESH
        ).start()

    def wait(ref, sem):
        pltpu.make_async_copy(ref, ref, sem).wait()

    barrier = pltpu.get_barrier_semaphore()

    @pl.loop(1, N_CTX)
    def _(d):
        pl.semaphore_signal(barrier, inc=1, device_id={"ctx": lax.rem(c + d, N_CTX)}, device_id_type=MESH)

    @pl.loop(1, N_TP)
    def _(d):
        pl.semaphore_signal(barrier, inc=1, device_id={"tp": lax.rem(t + d, N_TP)}, device_id_type=MESH)

    loads = [
        pltpu.make_async_copy(wq_hbm, wq, load_sem.at[0]),
        pltpu.make_async_copy(hidden_hbm, hidden, load_sem.at[1]),
        pltpu.make_async_copy(kvw_hbm, kvw, load_sem.at[2]),
        pltpu.make_async_copy(pos_hbm, pos_all.at[c], load_sem.at[3]),
        pltpu.make_async_copy(inv_hbm, inv_ref, load_sem.at[4]),
    ]
    for load in loads:
        load.start()
    counts_all[c] = counts_ref[...]
    loads[0].wait()
    pl.semaphore_wait(barrier, N_CTX + N_TP - 2)

    @pl.loop(1, N_CTX)
    def _(d):
        send(counts_ref, counts_all.at[c], send_sem.at[0], info_sem.at[0], {"ctx": lax.rem(c + d, N_CTX)})

    source = lax.rem(z + xl, 2) == 0
    other = lax.rem(z + xl, 2)
    relay = other == 1
    halves, sides = (xh, 1 - xh), (xl, 1 - xl)
    one_way = {(0, 0): 0, (0, 1): 1}

    def w_block(r, jj, zz, u):
        return wall.at[halves[r] * 4 + zz // 2, sides[jj], co, pl.ds(u * 128, 128)]

    def w_send(block, device, sem):
        send(block, block, send_sem.at[1], sem, device)

    def ring_sem(r, jj, way, slot, u):
        return w_sem.at[(((r * 2 + jj) * 2 + way) * 2 + slot) * 2 + u]

    def w_start(r, jj, u):
        block = w_block(r, jj, z, u)
        for way in range(2):
            w_send(block, z_near[way], ring_sem(r, jj, way, 0, u))
        w_send(block, far_x, w_far.at[jj])
        w_send(block, sibling, w_sib.at[0])

    def from_z(way, distance):
        return lax.rem(z + 8 - distance, 8) if way == 0 else lax.rem(z + distance, 8)

    def w_slot(r, jj, way, slot, ways):
        for u in range(2):
            block = w_block(r, jj, from_z(way, 2 + 2 * slot - other), u)
            wait(block, ring_sem(r, jj, way, slot, u))
            if way in ways:
                w_send(block, z_near[way], ring_sem(r, jj, way, 1 - other if slot == 0 else 1, u))
            w_send(block, far_x, w_far.at[jj])
            w_send(block, sibling, w_sib.at[0])

    def w_first(r, jj):
        for way in range(2):
            w_slot(r, jj, way, 0, (0, 1))

    def w_first_if(condition, r, jj):
        @pl.when(condition)
        def _():
            w_first(r, jj)

    def w_second_if(condition, r, jj):
        @pl.when(condition)
        def _():
            if condition is source:
                w_slot(r, jj, one_way[r, jj], 1, ())
            else:
                for way in range(2):
                    w_slot(r, jj, way, 1, (one_way[r, jj],))

    def w_second(r, jj):
        @pl.when(source)
        def _():
            w_slot(r, jj, one_way[r, jj], 1, ())

        @pl.when(jnp.logical_not(source))
        def _():
            for way in range(2):
                w_slot(r, jj, way, 1, (one_way[r, jj],))

    @pl.when(source)
    def _():
        wall[xh * 4 + z // 2, xl, co] = wq[...]
        for u in range(2):
            w_start(0, 0, u)
        for u in range(2):
            wait(w_block(0, 1, z, u), w_sem.at[32 + u])
            w_start(0, 1, u)
        w_first(0, 0)

    @pl.when(jnp.logical_not(source))
    def _():
        for u in range(2):
            rows_u = pl.ds(u * 128, 128)
            send(wq.at[rows_u], wall.at[xh * 4 + z // 2, xl, co, rows_u], send_sem.at[1], w_sem.at[32 + u], near_x)
        w_first(0, 0)
        w_first(0, 1)

    loads[3].wait()

    @pl.loop(1, N_CTX)
    def _(d):
        send(pos_all.at[c], pos_all.at[c], send_sem.at[8], pos_sem.at[0], {"ctx": lax.rem(c + d, N_CTX)})

    wait(counts_all.at[pl.ds(0, N_CTX - 1)], info_sem.at[0])
    counts = counts_all[...].reshape(N_CTX, 128)
    shard = iota((N_CTX, 128), 0)
    own_offset = jnp.sum(jnp.where(shard < c, counts, 0), axis=0, keepdims=True)
    slot = iota((1, CAP), 1)
    place = ((slot + jnp.concatenate([own_offset] * 3, axis=1)) % 32) * 16 + slot // 32
    loads[1].wait()
    for part in range(4):
        chosen = (iota((128, CAP), 0) + 128 * part == place).astype(F32).astype(BF16)
        moved = jnp.dot(chosen, hidden[...], preferred_element_type=F32).reshape(8, 16, 512)
        for k in range(4):
            tall = moved[:, :12, k * 128:(k + 1) * 128]
            outb[pl.ds(part * 8, 8), k * 12:(k + 1) * 12, :] = tall.astype(BF16)
    inb[c] = outb[c]

    @pl.loop(1, N_CTX)
    def _(d):
        peer = lax.rem(c + d, N_CTX)
        send(outb.at[peer], inb.at[c], send_sem.at[2], a2a_sem.at[0], {"ctx": peer})

    column = iota((1, 1536), 1)
    column_shard = (column * 1366) >> 16
    in_shard = column - column_shard * 48
    column_part = (in_shard * 5462) >> 16
    column_turn = in_shard - column_part * 12
    counts_wide = jnp.concatenate([counts] * 12, axis=1)
    shard_wide = iota((N_CTX, 1536), 0)
    first = jnp.sum(jnp.where(shard_wide < column_shard, counts_wide, 0), axis=0, keepdims=True)
    number = jnp.sum(jnp.where(shard_wide == column_shard, counts_wide, 0), axis=0, keepdims=True)
    low_rank = first + 32 * column_turn
    high_rank = jnp.minimum(low_rank + 32, first + number)
    pick_rank = iota((ROWS_DEV, 1536), 0) * N_CTX + c
    pick = (pick_rank >= low_rank) & (pick_rank < high_rank)
    loads[4].wait()
    wait(pos_all.at[pl.ds(0, N_CTX - 1)], pos_sem.at[0])
    lane = iota((N_CTX, 128), 1)
    first_of = jnp.sum(jnp.where(shard < lane, counts, 0), axis=0, keepdims=True)
    number_of = jnp.sum(jnp.where(shard == lane, counts, 0), axis=0, keepdims=True)
    rank = iota((ROWS_DEV, 128), 0) * N_CTX + c
    from_shard = (rank >= first_of) & (rank < first_of + number_of)
    within = jnp.sum(jnp.where(from_shard, rank - first_of, 0).astype(F32), axis=1, keepdims=True)
    holder = from_shard.astype(F32).astype(BF16)[:, :N_CTX]
    picked = jnp.zeros((ROWS_DEV, 128), F32)
    for part in range(3):
        place_of = pos_all[:, part, :]
        high = jnp.dot(holder, (place_of // 256).astype(F32).astype(BF16), preferred_element_type=F32)
        low = jnp.dot(holder, (place_of % 256).astype(F32).astype(BF16), preferred_element_type=F32)
        here = iota((ROWS_DEV, 128), 1).astype(F32) + 128.0 * part == within
        picked += jnp.where(here, high * 256.0 + low, 0.0)
    angles = jnp.sum(picked, axis=1, keepdims=True) * inv_ref[0:1, :]
    trig[0] = jnp.cos(angles)
    trig[1] = jnp.where(iota((ROWS_DEV, 128), 1) < HEAD_SIZE // 2, -1.0, 1.0) * jnp.sin(angles)

    wait(inb.at[pl.ds(0, N_CTX - 1)], a2a_sem.at[0])
    arrived = inb[...].reshape(1536, 128)
    for k in range(4):
        chosen = (pick & (column_part == k)).astype(F32).astype(BF16)
        xall[y, :, k * 128:(k + 1) * 128] = jnp.dot(chosen, arrived, preferred_element_type=F32).astype(BF16)

    def x_send(ref, device, sem):
        send(ref, ref, send_sem.at[3], sem, device)

    def x_part(yy, u):
        return xall.at[yy, pl.ds(u * 64, 64)]

    for u in range(2):
        x_send(x_part(y, u), y_right, x_sem.at[u])
        x_send(x_part(y, u), y_left, x_sem.at[8 + u])

    def x_step(s):
        for u in range(2):
            for way, device in ((0, y_right), (1, y_left)):
                if s == 3 and u != way:
                    continue
                part = x_part(lax.rem(y + (7 - s if way == 0 else 1 + s), 8), u)
                wait(part, x_sem.at[way * 8 + s * 2 + u])
                if s < 2 or (s == 2 and u == way):
                    x_send(part, device, x_sem.at[way * 8 + (s + 1) * 2 + u])

    loads[2].wait()
    rows = xall[y]
    for g in range(KEY_VALUE_HEADS):
        partial = jnp.dot(rows, kvw[:, g * 256:(g + 1) * 256], preferred_element_type=F32)
        for quarter in range(4):
            piece = partial[quarter * 32:(quarter + 1) * 32]
            kvfull[quarter % 2, g * 2 + quarter // 2] = piece
            kvp[quarter % 2, g * 2 + quarter // 2] = piece.astype(BF16)
    send(kvp.at[1 - xl], kvx, send_sem.at[4], rs_sem.at[0], near_x)

    def rotate(u, cosine, sine):
        return u * cosine + pltpu.roll(u, HEAD_SIZE // 2, 1) * sine

    own_kv = kvall.at[m, co, idx]
    z_half = z // 4

    def kv_where(n):
        return halves[n // 2], z_half if n % 2 == 0 else 1 - z_half

    def kv_send(ref, device, sem):
        send(ref, ref, send_sem.at[7], sem, device)

    mx, my, mxy = m + 1 - 2 * xl, lax.rem(m + 2, 4), 3 - m

    def kv_chunk(b, n):
        hh, half_z = kv_where(n)
        return kvall.at[b, co, pl.ds(pl.multiple_of(hh * 8 + half_z * 4, 4), 4)]

    def kv_out(n):
        wait(kvall.at[m, co, pl.ds(0, 4 if n else 3)], kv_sem.at[n])
        block = kv_chunk(m, n)
        kv_send(block, y_pair, kv_sem.at[4 + n])
        kv_send(block, near_x, kv_sem.at[8 + n])
        kv_send(block, sibling, kv_sem.at[16])

    def kv_mid(n):
        block = kv_chunk(mx if n % 2 else my, n)
        wait(block, kv_sem.at[8 + n if n % 2 else 4 + n])
        kv_send(block, y_pair if n % 2 else near_x, kv_sem.at[12 + n])
        kv_send(block, sibling, kv_sem.at[16])

    def kv_last(n):
        for block, k in ((kv_chunk(my if n % 2 else mx, n), 4 + n if n % 2 else 8 + n), (kv_chunk(mxy, n), 12 + n)):
            wait(block, kv_sem.at[k])
            kv_send(block, sibling, kv_sem.at[16])

    def partial_queries(j):
        def add_block(k, acc):
            return acc + jnp.dot(xall[k], wall[k, j].reshape(512, 256), preferred_element_type=F32)

        return lax.fori_loop(0, 8, add_block, jnp.zeros((ROWS_DEV, 256), F32))

    w_first_if(source, 0, 1)
    w_second(0, 0)
    wait(kvx, rs_sem.at[0])
    kvs[...] = (kvfull[xl] + kvx[...].astype(F32)).astype(BF16)
    kvin[y] = kvs[y]

    @pl.loop(1, 8)
    def _(d):
        peer = lax.rem(y + d, 8)
        send(kvs.at[peer], kvin.at[y], send_sem.at[5], rs_sem.at[1], {"tp": peer * 2 + xl})

    x_step(0)
    w_second(0, 1)
    x_step(1)
    mine_kv = pl.ds(pl.multiple_of(m * 32, 32), 32)
    wait(kvin.at[pl.ds(0, 7)], rs_sem.at[1])
    total = jnp.zeros((32, 256), F32)
    for s in range(8):
        total += kvin[s].astype(F32)
    kvall[m, co, idx, :, :HEAD_SIZE] = rotate(total[:, :HEAD_SIZE], trig[0, mine_kv], trig[1, mine_kv]).astype(BF16)
    kvall[m, co, idx, :, HEAD_SIZE:] = total[:, HEAD_SIZE:].astype(BF16)

    for n in range(4):
        hh, half_z = kv_where(n)

        @pl.loop(1 if n == 0 else 0, 4)
        def _(d):
            send(own_kv, own_kv, send_sem.at[6], kv_sem.at[n], ctx_of(hh, half_z * 4 + lax.rem(z + d, 4), co))

    x_step(2)
    kv_out(0)
    kv_out(1)
    kv_mid(0)
    wait(wall.at[pl.ds(0, 1)], w_far.at[0])
    w_send(wall.at[pl.ds((1 - xh) * 4, 4), sides[0], co], sibling, w_sib.at[0])
    wait(wall.at[pl.ds(0, 1)], w_far.at[1])
    w_send(wall.at[pl.ds((1 - xh) * 4, 4), sides[1], co], sibling, w_sib.at[0])
    kv_out(2)
    kv_mid(1)
    kv_out(3)
    x_step(3)
    kv_mid(2)
    wait(wall.at[pl.ds(0, 4)], w_sib.at[0])
    qpart[...] = partial_queries(1 - xl).astype(BF16)
    send(qpart, qin, send_sem.at[9], q_sem.at[0], near_x)
    kv_last(0)
    kv_mid(3)
    kv_last(1)
    q = partial_queries(xl)
    kv_last(2)
    kv_last(3)
    wait(qin, q_sem.at[0])
    q = q + qin[...].astype(F32)
    for head in range(2):
        turned = rotate(q[:, head * 128:(head + 1) * 128], trig[0], trig[1]).astype(BF16)
        for j in range(4):
            qbuf[j, head * 32:(head + 1) * 32, :] = turned[j * 32:(j + 1) * 32]

    wait(kvall.at[pl.ds(0, 2)], kv_sem.at[16])

    scale = 1.0 / math.sqrt(HEAD_SIZE)
    key_index = iota((64, 1024), 1)
    query_row = iota((64, 1024), 0) % 32
    key_row = key_index % 32
    key_ctx = (key_index // 32 % 16) * 2 + key_index // 512
    seen = (key_row < query_row) | ((key_row == query_row) & (key_ctx <= c))
    for j in range(4):
        scores = []
        for b in range(j + 1):
            keys = kvall[b, :, :, :, :HEAD_SIZE].reshape(1024, HEAD_SIZE)
            part = lax.dot_general(qbuf[j], keys, (((1,), (1,)), ((), ())), preferred_element_type=F32) * scale
            scores.append(jnp.where(seen, part, masked_score) if b == j else part)
        largest = jnp.max(scores[0], axis=1, keepdims=True)
        for part in scores[1:]:
            largest = jnp.maximum(largest, jnp.max(part, axis=1, keepdims=True))
        sums = jnp.zeros((64, 1), F32)
        mixed = jnp.zeros((64, HEAD_SIZE), F32)
        for b in range(j + 1):
            weights = jnp.exp(scores[b] - largest)
            if b == j:
                weights = jnp.where(seen, weights, 0.0)
            sums += jnp.sum(weights, axis=1, keepdims=True)
            values = kvall[b, :, :, :, HEAD_SIZE:].reshape(1024, HEAD_SIZE)
            mixed += jnp.dot(weights.astype(BF16), values, preferred_element_type=F32)
        result = (mixed / sums).astype(BF16)
        for head in range(2):
            out_ref[j * 32:(j + 1) * 32, head * 128:(head + 1) * 128] = result[head * 32:(head + 1) * 32]

    wait(counts_all.at[pl.ds(0, N_CTX - 1)], send_sem.at[0])

    @pl.when(source)
    def _():
        wait(wall, send_sem.at[1])

    @pl.when(jnp.logical_not(source))
    def _():
        wait(wall.at[pl.ds(0, 7)], send_sem.at[1])
        wait(wall.at[0, pl.ds(0, 1)], send_sem.at[1])
        wait(wq, send_sem.at[1])

    wait(inb.at[pl.ds(0, N_CTX - 1)], send_sem.at[2])
    wait(xall.at[pl.ds(0, 7)], send_sem.at[3])
    wait(kvx, send_sem.at[4])
    wait(kvin.at[pl.ds(0, 7)], send_sem.at[5])
    wait(kvall.at[m, co, pl.ds(0, 15)], send_sem.at[6])
    wait(kvall.at[pl.ds(0, 3)], send_sem.at[7])
    wait(kvall.at[m, co], send_sem.at[7])
    wait(pos_all.at[pl.ds(0, N_CTX - 1)], send_sem.at[8])
    wait(qin, send_sem.at[9])


def on_device(hidden, counts, positions, w_query, key_value_weight):
    exponent = np.arange(HEAD_SIZE // 2, dtype=np.float32) * np.float32(2.0 / HEAD_SIZE)
    inverse = np.power(np.float64(rope_base), -exponent.astype(np.float64)).astype(np.float32)
    inverse = jnp.asarray(np.tile(inverse, (8, 2)))
    vmem, hbm = pl.BlockSpec(memory_space=pltpu.VMEM), pl.BlockSpec(memory_space=pltpu.HBM)
    dma = pltpu.SemaphoreType.DMA
    return pl.pallas_call(
        kernel,
        out_shape=jax.ShapeDtypeStruct((ROWS_DEV, 256), BF16),
        in_specs=[vmem, hbm, hbm, hbm, hbm, hbm],
        out_specs=vmem,
        scratch_shapes=[
            pltpu.VMEM((N_CTX, 1, 128), jnp.int32),
            pltpu.VMEM((N_CTX, 3, 128), jnp.int32),
            pltpu.VMEM((8, 128), F32),
            pltpu.VMEM((CAP, 512), BF16),
            pltpu.VMEM((512, 1024), BF16),
            pltpu.VMEM((256, 256), BF16),
            pltpu.VMEM((N_CTX, 48, 128), BF16),
            pltpu.VMEM((N_CTX, 48, 128), BF16),
            pltpu.VMEM((8, ROWS_DEV, 512), BF16),
            pltpu.VMEM((8, 2, 2, 256, 256), BF16),
            pltpu.VMEM((2, 8, 32, 256), F32),
            pltpu.VMEM((2, 8, 32, 256), BF16),
            pltpu.VMEM((8, 32, 256), BF16),
            pltpu.VMEM((8, 32, 256), BF16),
            pltpu.VMEM((8, 32, 256), BF16),
            pltpu.VMEM((4, 2, 16, 32, 256), BF16),
            pltpu.VMEM((2, ROWS_DEV, 128), F32),
            pltpu.VMEM((ROWS_DEV, 256), BF16),
            pltpu.VMEM((ROWS_DEV, 256), BF16),
            pltpu.VMEM((4, 64, 128), BF16),
            dma((5,)),
            dma((10,)),
            dma((1,)),
            dma((1,)),
            dma((1,)),
            dma((34,)),
            dma((2,)),
            dma((1,)),
            dma((16,)),
            dma((2,)),
            dma((17,)),
            dma((1,)),
        ],
        compiler_params=pltpu.CompilerParams(
            collective_id=0, has_side_effects=True, vmem_limit_bytes=63 * 1024 * 1024
        ),
        name="gqa",
    )(
        jnp.broadcast_to(counts[:, None], (1, 128)), inverse, positions.reshape(3, 128),
        hidden, w_query, key_value_weight,
    )


def solution(mesh):
    return jax.shard_map(
        on_device,
        mesh=mesh,
        in_specs=(P("ctx", "tp"), P("ctx"), P("ctx"), P("ctx", "tp"), P("tp", None)),
        out_specs=P("ctx", "tp"),
        check_vma=False,
    )
```

time: 89.7 us -> 79.6 us (0.89)
  Pallas kernels: 84.1 us -> 76.7 us
  local copies, waits for them, and re-layouts: 4.5 us -> 2.02 us
    pallas_call x1, Pallas kernels: 84.1 us -> 76.7 us  [on_device(): pl.pallas_call(kernel, out_shape=jax.ShapeDtypeStruct((ROWS_DEV, 256), BF...]
    unnamed x9 -> x1, local copies, waits for them, and re-layouts: 4.35 us -> 1.47 us
where the time goes in v2:
time: 79.6 us; the launch traced here: 79.4 us
  Pallas kernels  76.7 us (96%)
  local copies, waits for them, and re-layouts  2.02 us (3%)
    pallas_call x1, Pallas kernels, on_device(): pl.pallas_call(kernel, out_shape=jax.ShapeDtypeStruct((ROWS_DEV, 256), BF...  76.7 us

profile of v2, /device:TPU:1, one launch (start us, length us, event | category | flops | bytes accessed | tf_op | source)
XLA Modules:
  0.0 79.4 jit_solution(5927438641482661634)
XLA Ops:
  0.7 0.5 broadcast_in_dim.9.counts_ref
  1.2 76.7 %gqa.1 = bf16[128,256]{1,0:T(8,128)(2,1)} custom-call(s32[1,128]{1,0:T(1,128)} %broadcast_in_dim.9.counts_ref, f32[8,128]{1,0:T(8,128)} %constant.2.clone.inv_hbm, s32[3,128]{1,0:T(4,128)} %bitcast.3, bf16[384,512]{1,0:T(8,128)(2,1)} %hidden_hbm.1, bf16[256,256]{1,0:T(8,128)(2,1)} %wq_hbm.1, bf16[512,1024]{1,0:T(8,128)(2,1)} %kvw_hbm.1), custom_call_target="tpu_custom_call" | custom-call | tf_op jit(solution)/shard_map/gqa/pallas_call | solution.py:418
  77.9 1.5 %copy.9 = bf16[128,256]{1,0:T(8,128)(2,1)} copy(bf16[128,256]{1,0:T(8,128)(2,1)} %gqa.1) | data formatting | bytes 131072

commit v3 on v2

--- a/solution.py
+++ b/solution.py
@@ -254,7 +254,9 @@
             piece = partial[quarter * 32:(quarter + 1) * 32]
             kvfull[quarter % 2, g * 2 + quarter // 2] = piece
             kvp[quarter % 2, g * 2 + quarter // 2] = piece.astype(BF16)
-    send(kvp.at[1 - xl], kvx, send_sem.at[4], rs_sem.at[0], near_x)
+    for h in range(2):
+        part = pl.ds(h * 4, 4)
+        send(kvp.at[1 - xl, part], kvx.at[part], send_sem.at[4], rs_sem.at[h], near_x)
 
     def rotate(u, cosine, sine):
         return u * cosine + pltpu.roll(u, HEAD_SIZE // 2, 1) * sine
@@ -296,24 +298,38 @@
         def add_block(k, acc):
             return acc + jnp.dot(xall[k], wall[k, j].reshape(512, 256), preferred_element_type=F32)
 
-        return lax.fori_loop(0, 8, add_block, jnp.zeros((ROWS_DEV, 256), F32))
+        return lax.fori_loop(0, 8, add_block, jnp.zeros((ROWS_DEV, 256), F32), unroll=True)
 
     w_first_if(source, 0, 1)
     w_second(0, 0)
-    wait(kvx, rs_sem.at[0])
-    kvs[...] = (kvfull[xl] + kvx[...].astype(F32)).astype(BF16)
-    kvin[y] = kvs[y]
-
-    @pl.loop(1, 8)
-    def _(d):
-        peer = lax.rem(y + d, 8)
-        send(kvs.at[peer], kvin.at[y], send_sem.at[5], rs_sem.at[1], {"tp": peer * 2 + xl})
+    wait(kvx.at[pl.ds(0, 4)], rs_sem.at[0])
+    kvs[0:4] = (kvfull[xl, 0:4] + kvx[0:4].astype(F32)).astype(BF16)
+
+    def kvs_send(peer):
+        @pl.when(peer == y)
+        def _():
+            kvin[y] = kvs[y]
+
+        @pl.when(peer != y)
+        def _():
+            send(kvs.at[peer], kvin.at[y], send_sem.at[5], rs_sem.at[2], {"tp": peer * 2 + xl})
+
+    @pl.loop(0, 4)
+    def _(d):
+        kvs_send(lax.rem(y + d, 4))
+
+    wait(kvx.at[pl.ds(4, 4)], rs_sem.at[1])
+    kvs[4:8] = (kvfull[xl, 4:8] + kvx[4:8].astype(F32)).astype(BF16)
+
+    @pl.loop(0, 4)
+    def _(d):
+        kvs_send(4 + lax.rem(y + d, 4))
 
     x_step(0)
     w_second(0, 1)
     x_step(1)
     mine_kv = pl.ds(pl.multiple_of(m * 32, 32), 32)
-    wait(kvin.at[pl.ds(0, 7)], rs_sem.at[1])
+    wait(kvin.at[pl.ds(0, 7)], rs_sem.at[2])
     total = jnp.zeros((32, 256), F32)
     for s in range(8):
         total += kvin[s].astype(F32)
@@ -450,7 +466,7 @@
             dma((2,)),
             dma((1,)),
             dma((16,)),
-            dma((2,)),
+            dma((3,)),
             dma((17,)),
             dma((1,)),
         ],

time: 79.6 us -> 79.1 us (level)
  no operation moved by 1% of the time
where the time goes in v3:
time: 79.1 us; the launch traced here: 78.9 us
  Pallas kernels  76.2 us (96%)
  local copies, waits for them, and re-layouts  2.02 us (3%)
    pallas_call x1, Pallas kernels, on_device(): pl.pallas_call(kernel, out_shape=jax.ShapeDtypeStruct((ROWS_DEV, 256), BF...  76.2 us

profile of v3, /device:TPU:1, one launch (start us, length us, event | category | flops | bytes accessed | tf_op | source)
XLA Modules:
  0.0 78.9 jit_solution(621229421523599125)
XLA Ops:
  0.7 0.5 broadcast_in_dim.9.counts_ref
  1.2 76.2 %gqa.1 = bf16[128,256]{1,0:T(8,128)(2,1)} custom-call(s32[1,128]{1,0:T(1,128)} %broadcast_in_dim.9.counts_ref, f32[8,128]{1,0:T(8,128)} %constant.2.clone.inv_hbm, s32[3,128]{1,0:T(4,128)} %bitcast.3, bf16[384,512]{1,0:T(8,128)(2,1)} %hidden_hbm.1, bf16[256,256]{1,0:T(8,128)(2,1)} %wq_hbm.1, bf16[512,1024]{1,0:T(8,128)(2,1)} %kvw_hbm.1), custom_call_target="tpu_custom_call" | custom-call | tf_op jit(solution)/shard_map/gqa/pallas_call | solution.py:434
  77.4 1.5 %copy.9 = bf16[128,256]{1,0:T(8,128)(2,1)} copy(bf16[128,256]{1,0:T(8,128)(2,1)} %gqa.1) | data formatting | bytes 131072

commit v4 on v3

--- a/solution.py
+++ b/solution.py
@@ -160,12 +160,6 @@
             send(wq.at[rows_u], wall.at[xh * 4 + z // 2, xl, co, rows_u], send_sem.at[1], w_sem.at[32 + u], near_x)
         w_first(0, 0)
         w_first(0, 1)
-
-    loads[3].wait()
-
-    @pl.loop(1, N_CTX)
-    def _(d):
-        send(pos_all.at[c], pos_all.at[c], send_sem.at[8], pos_sem.at[0], {"ctx": lax.rem(c + d, N_CTX)})
 
     wait(counts_all.at[pl.ds(0, N_CTX - 1)], info_sem.at[0])
     counts = counts_all[...].reshape(N_CTX, 128)
@@ -187,6 +181,12 @@
         peer = lax.rem(c + d, N_CTX)
         send(outb.at[peer], inb.at[c], send_sem.at[2], a2a_sem.at[0], {"ctx": peer})
 
+    loads[3].wait()
+
+    @pl.loop(1, N_CTX)
+    def _(d):
+        send(pos_all.at[c], pos_all.at[c], send_sem.at[8], pos_sem.at[0], {"ctx": lax.rem(c + d, N_CTX)})
+
     column = iota((1, 1536), 1)
     column_shard = (column * 1366) >> 16
     in_shard = column - column_shard * 48
@@ -200,6 +200,114 @@
     high_rank = jnp.minimum(low_rank + 32, first + number)
     pick_rank = iota((ROWS_DEV, 1536), 0) * N_CTX + c
     pick = (pick_rank >= low_rank) & (pick_rank < high_rank)
+    wait(inb.at[pl.ds(0, N_CTX - 1)], a2a_sem.at[0])
+    arrived = inb[...].reshape(1536, 128)
+    for k in range(4):
+        chosen = (pick & (column_part == k)).astype(F32).astype(BF16)
+        xall[y, :, k * 128:(k + 1) * 128] = jnp.dot(chosen, arrived, preferred_element_type=F32).astype(BF16)
+
+    def x_send(ref, device, sem):
+        send(ref, ref, send_sem.at[3], sem, device)
+
+    def x_part(yy, u):
+        return xall.at[yy, pl.ds(u * 64, 64)]
+
+    for u in range(2):
+        x_send(x_part(y, u), y_right, x_sem.at[u])
+        x_send(x_part(y, u), y_left, x_sem.at[8 + u])
+
+    def x_step(s):
+        for u in range(2):
+            for way, device in ((0, y_right), (1, y_left)):
+                if s == 3 and u != way:
+                    continue
+                part = x_part(lax.rem(y + (7 - s if way == 0 else 1 + s), 8), u)
+                wait(part, x_sem.at[way * 8 + s * 2 + u])
+                if s < 2 or (s == 2 and u == way):
+                    x_send(part, device, x_sem.at[way * 8 + (s + 1) * 2 + u])
+
+    loads[2].wait()
+    rows = xall[y]
+    for g in range(KEY_VALUE_HEADS):
+        partial = jnp.dot(rows, kvw[:, g * 256:(g + 1) * 256], preferred_element_type=F32)
+        for quarter in range(4):
+            piece = partial[quarter * 32:(quarter + 1) * 32]
+            kvfull[quarter % 2, g * 2 + quarter // 2] = piece
+            kvp[quarter % 2, g * 2 + quarter // 2] = piece.astype(BF16)
+    for h in range(2):
+        part = pl.ds(h * 4, 4)
+        send(kvp.at[1 - xl, part], kvx.at[part], send_sem.at[4], rs_sem.at[h], near_x)
+
+    def rotate(u, cosine, sine):
+        return u * cosine + pltpu.roll(u, HEAD_SIZE // 2, 1) * sine
+
+    own_kv = kvall.at[m, co, idx]
+    z_half = z // 4
+
+    def kv_where(n):
+        return halves[n // 2], z_half if n % 2 == 0 else 1 - z_half
+
+    def kv_send(ref, device, sem):
+        send(ref, ref, send_sem.at[7], sem, device)
+
+    mx, my, mxy = m + 1 - 2 * xl, lax.rem(m + 2, 4), 3 - m
+
+    def kv_chunk(b, n):
+        hh, half_z = kv_where(n)
+        return kvall.at[b, co, pl.ds(pl.multiple_of(hh * 8 + half_z * 4, 4), 4)]
+
+    def kv_out(n):
+        wait(kvall.at[m, co, pl.ds(0, 4 if n else 3)], kv_sem.at[n])
+        block = kv_chunk(m, n)
+        kv_send(block, y_pair, kv_sem.at[4 + n])
+        kv_send(block, near_x, kv_sem.at[8 + n])
+        kv_send(block, sibling, kv_sem.at[16])
+
+    def kv_mid(n):
+        block = kv_chunk(mx if n % 2 else my, n)
+        wait(block, kv_sem.at[8 + n if n % 2 else 4 + n])
+        kv_send(block, y_pair if n % 2 else near_x, kv_sem.at[12 + n])
+        kv_send(block, sibling, kv_sem.at[16])
+
+    def kv_last(n):
+        for block, k in ((kv_chunk(my if n % 2 else mx, n), 4 + n if n % 2 else 8 + n), (kv_chunk(mxy, n), 12 + n)):
+            wait(block, kv_sem.at[k])
+            kv_send(block, sibling, kv_sem.at[16])
+
+    def partial_queries(j):
+        def add_block(k, acc):
+            return acc + jnp.dot(xall[k], wall[k, j].reshape(512, 256), preferred_element_type=F32)
+
+        return lax.fori_loop(0, 8, add_block, jnp.zeros((ROWS_DEV, 256), F32), unroll=True)
+
+    w_first_if(source, 0, 1)
+    w_second(0, 0)
+    wait(kvx.at[pl.ds(0, 4)], rs_sem.at[0])
+    kvs[0:4] = (kvfull[xl, 0:4] + kvx[0:4].astype(F32)).astype(BF16)
+
+    def kvs_send(peer):
+        @pl.when(peer == y)
+        def _():
+            kvin[y] = kvs[y]
+
+        @pl.when(peer != y)
+        def _():
+            send(kvs.at[peer], kvin.at[y], send_sem.at[5], rs_sem.at[2], {"tp": peer * 2 + xl})
+
+    @pl.loop(0, 4)
+    def _(d):
+        kvs_send(lax.rem(y + d, 4))
+
+    wait(kvx.at[pl.ds(4, 4)], rs_sem.at[1])
+    kvs[4:8] = (kvfull[xl, 4:8] + kvx[4:8].astype(F32)).astype(BF16)
+
+    @pl.loop(0, 4)
+    def _(d):
+        kvs_send(4 + lax.rem(y + d, 4))
+
+    x_step(0)
+    w_second(0, 1)
+    x_step(1)
     loads[4].wait()
     wait(pos_all.at[pl.ds(0, N_CTX - 1)], pos_sem.at[0])
     lane = iota((N_CTX, 128), 1)
@@ -220,114 +328,6 @@
     trig[0] = jnp.cos(angles)
     trig[1] = jnp.where(iota((ROWS_DEV, 128), 1) < HEAD_SIZE // 2, -1.0, 1.0) * jnp.sin(angles)
 
-    wait(inb.at[pl.ds(0, N_CTX - 1)], a2a_sem.at[0])
-    arrived = inb[...].reshape(1536, 128)
-    for k in range(4):
-        chosen = (pick & (column_part == k)).astype(F32).astype(BF16)
-        xall[y, :, k * 128:(k + 1) * 128] = jnp.dot(chosen, arrived, preferred_element_type=F32).astype(BF16)
-
-    def x_send(ref, device, sem):
-        send(ref, ref, send_sem.at[3], sem, device)
-
-    def x_part(yy, u):
-        return xall.at[yy, pl.ds(u * 64, 64)]
-
-    for u in range(2):
-        x_send(x_part(y, u), y_right, x_sem.at[u])
-        x_send(x_part(y, u), y_left, x_sem.at[8 + u])
-
-    def x_step(s):
-        for u in range(2):
-            for way, device in ((0, y_right), (1, y_left)):
-                if s == 3 and u != way:
-                    continue
-                part = x_part(lax.rem(y + (7 - s if way == 0 else 1 + s), 8), u)
-                wait(part, x_sem.at[way * 8 + s * 2 + u])
-                if s < 2 or (s == 2 and u == way):
-                    x_send(part, device, x_sem.at[way * 8 + (s + 1) * 2 + u])
-
-    loads[2].wait()
-    rows = xall[y]
-    for g in range(KEY_VALUE_HEADS):
-        partial = jnp.dot(rows, kvw[:, g * 256:(g + 1) * 256], preferred_element_type=F32)
-        for quarter in range(4):
-            piece = partial[quarter * 32:(quarter + 1) * 32]
-            kvfull[quarter % 2, g * 2 + quarter // 2] = piece
-            kvp[quarter % 2, g * 2 + quarter // 2] = piece.astype(BF16)
-    for h in range(2):
-        part = pl.ds(h * 4, 4)
-        send(kvp.at[1 - xl, part], kvx.at[part], send_sem.at[4], rs_sem.at[h], near_x)
-
-    def rotate(u, cosine, sine):
-        return u * cosine + pltpu.roll(u, HEAD_SIZE // 2, 1) * sine
-
-    own_kv = kvall.at[m, co, idx]
-    z_half = z // 4
-
-    def kv_where(n):
-        return halves[n // 2], z_half if n % 2 == 0 else 1 - z_half
-
-    def kv_send(ref, device, sem):
-        send(ref, ref, send_sem.at[7], sem, device)
-
-    mx, my, mxy = m + 1 - 2 * xl, lax.rem(m + 2, 4), 3 - m
-
-    def kv_chunk(b, n):
-        hh, half_z = kv_where(n)
-        return kvall.at[b, co, pl.ds(pl.multiple_of(hh * 8 + half_z * 4, 4), 4)]
-
-    def kv_out(n):
-        wait(kvall.at[m, co, pl.ds(0, 4 if n else 3)], kv_sem.at[n])
-        block = kv_chunk(m, n)
-        kv_send(block, y_pair, kv_sem.at[4 + n])
-        kv_send(block, near_x, kv_sem.at[8 + n])
-        kv_send(block, sibling, kv_sem.at[16])
-
-    def kv_mid(n):
-        block = kv_chunk(mx if n % 2 else my, n)
-        wait(block, kv_sem.at[8 + n if n % 2 else 4 + n])
-        kv_send(block, y_pair if n % 2 else near_x, kv_sem.at[12 + n])
-        kv_send(block, sibling, kv_sem.at[16])
-
-    def kv_last(n):
-        for block, k in ((kv_chunk(my if n % 2 else mx, n), 4 + n if n % 2 else 8 + n), (kv_chunk(mxy, n), 12 + n)):
-            wait(block, kv_sem.at[k])
-            kv_send(block, sibling, kv_sem.at[16])
-
-    def partial_queries(j):
-        def add_block(k, acc):
-            return acc + jnp.dot(xall[k], wall[k, j].reshape(512, 256), preferred_element_type=F32)
-
-        return lax.fori_loop(0, 8, add_block, jnp.zeros((ROWS_DEV, 256), F32), unroll=True)
-
-    w_first_if(source, 0, 1)
-    w_second(0, 0)
-    wait(kvx.at[pl.ds(0, 4)], rs_sem.at[0])
-    kvs[0:4] = (kvfull[xl, 0:4] + kvx[0:4].astype(F32)).astype(BF16)
-
-    def kvs_send(peer):
-        @pl.when(peer == y)
-        def _():
-            kvin[y] = kvs[y]
-
-        @pl.when(peer != y)
-        def _():
-            send(kvs.at[peer], kvin.at[y], send_sem.at[5], rs_sem.at[2], {"tp": peer * 2 + xl})
-
-    @pl.loop(0, 4)
-    def _(d):
-        kvs_send(lax.rem(y + d, 4))
-
-    wait(kvx.at[pl.ds(4, 4)], rs_sem.at[1])
-    kvs[4:8] = (kvfull[xl, 4:8] + kvx[4:8].astype(F32)).astype(BF16)
-
-    @pl.loop(0, 4)
-    def _(d):
-        kvs_send(4 + lax.rem(y + d, 4))
-
-    x_step(0)
-    w_second(0, 1)
-    x_step(1)
     mine_kv = pl.ds(pl.multiple_of(m * 32, 32), 32)
     wait(kvin.at[pl.ds(0, 7)], rs_sem.at[2])
     total = jnp.zeros((32, 256), F32)

time: 79.1 us -> 80 us (1.011)
  Pallas kernels: 76.2 us -> 77.1 us
    pallas_call x1, Pallas kernels: 76.2 us -> 77.1 us  [on_device(): pl.pallas_call(kernel, out_shape=jax.ShapeDtypeStruct((ROWS_DEV, 256), BF...]
where the time goes in v4:
time: 80 us; the launch traced here: 79.8 us
  Pallas kernels  77.1 us (96%)
  local copies, waits for them, and re-layouts  2.02 us (3%)
    pallas_call x1, Pallas kernels, on_device(): pl.pallas_call(kernel, out_shape=jax.ShapeDtypeStruct((ROWS_DEV, 256), BF...  77.1 us

profile of v4, /device:TPU:1, one launch (start us, length us, event | category | flops | bytes accessed | tf_op | source)
XLA Modules:
  0.0 79.8 jit_solution(11659526231014799710)
XLA Ops:
  0.7 0.5 broadcast_in_dim.9.counts_ref
  1.2 77.1 %gqa.1 = bf16[128,256]{1,0:T(8,128)(2,1)} custom-call(s32[1,128]{1,0:T(1,128)} %broadcast_in_dim.9.counts_ref, f32[8,128]{1,0:T(8,128)} %constant.2.clone.inv_hbm, s32[3,128]{1,0:T(4,128)} %bitcast.3, bf16[384,512]{1,0:T(8,128)(2,1)} %hidden_hbm.1, bf16[256,256]{1,0:T(8,128)(2,1)} %wq_hbm.1, bf16[512,1024]{1,0:T(8,128)(2,1)} %kvw_hbm.1), custom_call_target="tpu_custom_call" | custom-call | tf_op jit(solution)/shard_map/gqa/pallas_call | solution.py:434
  78.3 1.5 %copy.9 = bf16[128,256]{1,0:T(8,128)(2,1)} copy(bf16[128,256]{1,0:T(8,128)(2,1)} %gqa.1) | data formatting | bytes 131072
